TPU v7x, 32 devices: a whole 2x2x4 slice. The times are simulated.
32 devices in a mesh: route: 16 (over z, y, x), scen: 2 (over core).
Axes of the slice: x: 2, y: 2, z: 4, core: 2. Of those that a mesh axis runs over, the one named last changes fastest.
Arguments:
- starting_warming: float32 [128, 16, 512], P('route', 'scen'), may hold values from -6 to 6
- schur_reciprocal: float32 [4, 512, 512], replicated, may hold values from -1 to 1
- ground_level_group: int32 [128], P('route'), may hold values from 0 to 3
- link_coefficient: float32 [128, 128], P('route'), may hold values from 40 to 16384
- dissipation_matrices: float32 [2, 128, 6, 512], P('scen', 'route'), may hold values from 0.05 to 1
- timestep_holder: int32 [2, 6], replicated, may hold values from 0 to 1
- current_demand: int32 [2, 6, 16], P(None, None, 'scen'), may hold values from 0 to 10
Outputs:
- temperatures: float32 [2, 128, 16, 512], P(None, 'route', 'scen')
All inputs are finite; a program needn't handle non-finite values.
Results may differ from a plain program's by a relative error of at most 0.0042.
Values sent between devices are 32-bit elements; how exact they have to be, the bound alone decides.
A program may use at most 64 MiB of HBM per device.

v0:
```python
import jax
import jax.numpy as jnp
from jax import lax
from jax.sharding import PartitionSpec as P

HOURS = 2


highest = lax.Precision.HIGHEST
clock_timestep = 1.0
level_step = 0.1


def spread(value, axis, source):
    kept = jnp.where(lax.axis_index(axis) == source, value, 0).astype(value.dtype)
    return lax.psum(kept, axis)


def carried_in(value, axis, join, neutral, backward):
    count, mine = (lax.axis_size(axis), lax.axis_index(axis))
    pieces = jax.tree.map(lambda part: lax.all_gather(part, axis), value)
    if backward:
        pieces = jax.tree.map(lambda part: part[::-1], pieces)
        mine = count - 1 - mine
    so_far = jax.tree.map(
        lambda part, zero: jnp.full_like(part, 0) + jnp.asarray(zero, part.dtype), value, neutral
    )

    def step(position, so_far):
        longer = join(so_far, jax.tree.map(lambda part: part[position], pieces))
        return jax.tree.map(lambda new, old: jnp.where(position < mine, new, old), longer, so_far)

    return lax.fori_loop(0, count - 1, step, so_far)


def compose(former, latter):
    joined = jnp.dot(former[0], latter[0], precision=highest)
    moved = jnp.dot(former[1], latter[0], precision=highest) + latter[1]
    return (joined, moved)


def shards(
    starting_warming,
    schur_reciprocal,
    ground_level_group,
    link_coefficient,
    dissipation_matrices,
    timestep_holder,
    current_demand,
):
    piece_within_device = starting_warming.shape[0]
    case_within_device = starting_warming.shape[1]
    core_width = link_coefficient.shape[1]
    circuit_count = dissipation_matrices.shape[2]
    inverse_low = schur_reciprocal.astype(jnp.bfloat16)
    low_inverses = [
        lax.dynamic_index_in_dim(inverse_low, ground_level_group[segment], 0, keepdims=False)
        for segment in range(piece_within_device)
    ]
    core_rows = [
        lax.dynamic_index_in_dim(schur_reciprocal, ground_level_group[segment], 0, keepdims=False)[
            :core_width
        ]
        for segment in range(piece_within_device)
    ]
    forward_steps = [
        link_coefficient[segment][:, None] * core_rows[segment][:, :core_width]
        for segment in range(piece_within_device)
    ]
    backward_steps = [
        core_rows[segment][:, :core_width] * link_coefficient[segment][None, :]
        for segment in range(piece_within_device)
    ]
    identity_mat = jnp.eye(core_width, dtype=jnp.float32)
    forward_total = identity_mat
    for segment in range(piece_within_device):
        forward_total = jnp.dot(forward_total, forward_steps[segment], precision=highest)
    backward_total = identity_mat
    for segment in reversed(range(piece_within_device)):
        backward_total = jnp.dot(backward_total, backward_steps[segment], precision=highest)
    empty_rows = jnp.zeros((case_within_device, core_width), jnp.float32)
    thermal_excess = starting_warming
    saved_entries = []
    for hour_step in range(HOURS):
        circuit_blocks = []
        for circuit in range(circuit_count):
            circuit_blocks.append(
                spread(
                    dissipation_matrices[0, :, circuit, :],
                    "scen",
                    timestep_holder[hour_step, circuit],
                )
            )
        blocks = jnp.stack(circuit_blocks, axis=1)
        current = current_demand[hour_step].astype(jnp.float32) * level_step
        power_input = jnp.sum((current * current)[None, :, :, None] * blocks[:, :, None, :], axis=1)
        applied_power = (thermal_excess + clock_timestep * power_input).astype(jnp.bfloat16)
        solved = [
            jnp.dot(
                applied_power[segment], low_inverses[segment], preferred_element_type=jnp.float32
            )
            for segment in range(piece_within_device)
        ]
        forward_tail = empty_rows
        for segment in range(piece_within_device):
            forward_tail = (
                jnp.dot(forward_tail, forward_steps[segment], precision=highest)
                + solved[segment][:, :core_width]
            )
        incoming = carried_in(
            (forward_total, forward_tail), "route", compose, (identity_mat, empty_rows), False
        )[1]
        lower_solve_lines = []
        running = incoming
        for segment in range(piece_within_device):
            row_block = solved[segment] + jnp.dot(
                link_coefficient[segment][None, :] * running, core_rows[segment], precision=highest
            )
            lower_solve_lines.append(row_block)
            running = row_block[:, :core_width]
        backward_tail = empty_rows
        for segment in reversed(range(piece_within_device)):
            backward_tail = (
                jnp.dot(backward_tail, backward_steps[segment], precision=highest)
                + link_coefficient[segment][None, :] * lower_solve_lines[segment][:, :core_width]
            )
        incoming_back = carried_in(
            (backward_total, backward_tail), "route", compose, (identity_mat, empty_rows), True
        )[1]
        timestep_outputs = [None] * piece_within_device
        running = incoming_back
        for segment in reversed(range(piece_within_device)):
            result = lower_solve_lines[segment] + jnp.dot(
                running, core_rows[segment], precision=highest
            )
            timestep_outputs[segment] = result
            running = link_coefficient[segment][None, :] * result[:, :core_width]
        thermal_excess = jnp.stack(timestep_outputs)
        saved_entries.append(thermal_excess)
    return jnp.stack(saved_entries)


def solution(mesh):
    return jax.shard_map(
        shards,
        mesh=mesh,
        in_specs=(
            P("route", "scen", None),
            P(),
            P("route"),
            P("route", None),
            P("scen", "route", None, None),
            P(),
            P(None, None, "scen"),
        ),
        out_specs=P(None, "route", "scen", None),
        check_vma=False,
    )
```

profile of v0, /device:TPU:0, one launch (start us, length us, event | category | flops | bytes accessed | tf_op | source)
XLA Modules:
  0.0 376.9 jit_solution(1320350301866201785)
XLA Ops:
  7.4 1.8 fusion.245
  16.8 1.4 select_bitcast_fusion.6
  18.1 1.5 select_bitcast_fusion
  19.7 1.6 fusion.246
  37.3 1.9 dynamic-slice_bitcast_fusion
  44.7 2.5 convert_element_type.41
  47.1 1.6 fusion.91
  48.7 1.7 fusion.90
  65.1 42.8 %all-gather.1 = f32[128,128]{1,0:T(8,128)S(1)} all-gather(f32[8,128]{1,0:T(8,128)S(1)} %convolution_add_fusion.53), channel_id=3, replica_groups=mesh['route'=16,'scen'=2] {'route'}, dimensions={0}, use_global_device_ids=true | all-gather | bytes 69632 | tf_op jit(solution)/shard_map/all_gather | solution.py:21
  108.7 2.3 rev.10
  111.0 46.1 %all-gather.9.cloned.1.call-done = f32[2048,128]{1,0:T(8,128)} async-done(((f32[128,128]{1,0:T(8,128)}), f32[2048,128]{1,0:T(8,128)}) %all-gather.9.cloned.1.call-update) | async-done | bytes 1048592 | tf_op jit(solution)/shard_map/all_gather | solution.py:21
  157.1 15.3 %while.56 = (s32[]{:T(128)}, f32[8,128]{1,0:T(8,128)S(1)}, s32[]{:T(128)}, f32[16,128,128]{2,1,0:T(8,128)}, f32[16,8,128]{2,1,0:T(8,128)S(1)}, /*index=5*/s32[]{:T(128)}, s32[]{:T(128)}) while((s32[]{:T(128)}, f32[8,128]{1,0:T(8,128)S(1)}, s32[]{:T(128)}, f32[16,128,128]{2,1,0:T(8,128)}, f32[16,8,128]{2,1,0:T(8,128)S(1)}, ...), condition=%wide.region_8.9_spmd.clone, body=%wide.region_7.8_spmd.clone.sunk | while | flops 1576964 | bytes 92775 | solution.py:33
  172.4 1.2 convolution_add_fusion.31
  178.5 1.2 convolution_add_fusion.25
  185.0 38.9 %all-gather.3 = f32[128,128]{1,0:T(8,128)S(1)} all-gather(f32[8,128]{1,0:T(8,128)S(1)} %convolution_add_fusion.46), channel_id=5, replica_groups=mesh['route'=16,'scen'=2] {'route'}, dimensions={0}, use_global_device_ids=true | all-gather | bytes 69632 | tf_op jit(solution)/shard_map/all_gather | solution.py:21
  224.5 15.3 %while.57 = (s32[]{:T(128)}, f32[8,128]{1,0:T(8,128)S(1)}, s32[]{:T(128)}, f32[16,128,128]{2,1,0:T(8,128)}, f32[16,8,128]{2,1,0:T(8,128)}, /*index=5*/s32[]{:T(128)}, s32[]{:T(128)}) while((s32[]{:T(128)}, f32[8,128]{1,0:T(8,128)S(1)}, s32[]{:T(128)}, f32[16,128,128]{2,1,0:T(8,128)}, f32[16,8,128]{2,1,0:T(8,128)}, ...), condition=%wide.region_10.11_spmd.clone, body=%wide.region_9.10_spmd.clone.sunk | while | flops 1576964 | bytes 92775 | solution.py:33
  239.8 1.3 convolution_add_fusion.23
  241.1 1.2 convolution_add_fusion.22
  252.6 35.9 %all-gather.4 = f32[128,128]{1,0:T(8,128)S(1)} all-gather(f32[8,128]{1,0:T(8,128)S(1)} %convolution_add_fusion.39), channel_id=6, replica_groups=mesh['route'=16,'scen'=2] {'route'}, dimensions={0}, use_global_device_ids=true | all-gather | bytes 69632 | tf_op jit(solution)/shard_map/all_gather | solution.py:21
  288.6 15.3 %while.58 = (s32[]{:T(128)}, f32[8,128]{1,0:T(8,128)S(1)}, s32[]{:T(128)}, f32[16,128,128]{2,1,0:T(8,128)}, f32[16,8,128]{2,1,0:T(8,128)S(1)}, /*index=5*/s32[]{:T(128)}, s32[]{:T(128)}) while((s32[]{:T(128)}, f32[8,128]{1,0:T(8,128)S(1)}, s32[]{:T(128)}, f32[16,128,128]{2,1,0:T(8,128)}, f32[16,8,128]{2,1,0:T(8,128)S(1)}, ...), condition=%wide.region_19.20_spmd.clone, body=%wide.region_18.19_spmd.clone.sunk | while | flops 1576964 | bytes 92775 | solution.py:33
  303.9 1.2 convolution_add_fusion.15
  310.0 1.2 convolution_add_fusion.9
  313.6 37.8 %all-gather.5 = f32[128,128]{1,0:T(8,128)S(1)} all-gather(f32[8,128]{1,0:T(8,128)S(1)} %convolution_add_fusion.32), channel_id=7, replica_groups=mesh['route'=16,'scen'=2] {'route'}, dimensions={0}, use_global_device_ids=true | all-gather | bytes 69632 | tf_op jit(solution)/shard_map/all_gather | solution.py:21
  351.4 15.3 %while.59 = (s32[]{:T(128)}, f32[8,128]{1,0:T(8,128)S(1)}, s32[]{:T(128)}, f32[16,128,128]{2,1,0:T(8,128)}, f32[16,8,128]{2,1,0:T(8,128)S(1)}, /*index=5*/s32[]{:T(128)}, s32[]{:T(128)}) while((s32[]{:T(128)}, f32[8,128]{1,0:T(8,128)S(1)}, s32[]{:T(128)}, f32[16,128,128]{2,1,0:T(8,128)}, f32[16,8,128]{2,1,0:T(8,128)S(1)}, ...), condition=%wide.region_21.22_spmd.clone, body=%wide.region_20.21_spmd.clone.sunk | while | flops 1576964 | bytes 92775 | solution.py:33
  (373 shorter events, 113.5 us)
Async XLA Ops:
  7.4 43.7 %all-reduce.3.cloned.1.call-start = ((), (), s32[]{:S(2)}) async-start(), calls=%async_computation.2 | async-start | bytes 393216 | tf_op jit(solution)/shard_map/psum | solution.py:16
  19.6 89.0 %all-gather.11.cloned.1.call-start = ((), (), s32[]{:S(2)}) async-start(), calls=%async_computation.1 | async-start | bytes 1114112 | tf_op jit(solution)/shard_map/all_gather | solution.py:21
  32.3 212.8 %copy-start.36 = (f32[128]{0:T(128)}, f32[128]{0:T(128)S(1)}, u32[]{:S(2)}) copy-start(f32[128]{0:T(128)S(1)} %get-tuple-element.534) | copy-start | bytes 1540
  32.3 213.1 %copy-start.33 = (f32[128]{0:T(128)}, f32[128]{0:T(128)S(1)}, u32[]{:S(2)}) copy-start(f32[128]{0:T(128)S(1)} %get-tuple-element.535) | copy-start | bytes 1540
  41.6 115.5 %all-gather.9.cloned.1.call-start = ((), (), s32[]{:S(2)}) async-start(), calls=%async_computation | async-start | bytes 1114112 | tf_op jit(solution)/shard_map/all_gather | solution.py:21
  60.5 48.2 %copy-start.14 = (f32[8,512]{1,0:T(8,128)}, f32[8,512]{1,0:T(8,128)S(1)}, u32[]{:S(2)}) copy-start(f32[8,512]{1,0:T(8,128)S(1)} %fusion.46) | copy-start | bytes 49156
  60.5 47.4 %copy-start.57 = (f32[6,8]{1,0:T(8,128)S(1)}, f32[6,8]{1,0:T(8,128)}, u32[]{:S(2)}) copy-start(f32[6,8]{1,0:T(8,128)} %get-tuple-element.561) | copy-start | bytes 580
  60.6 50.4 %copy-start.17 = (f32[8,512]{1,0:T(8,128)}, f32[8,512]{1,0:T(8,128)S(1)}, u32[]{:S(2)}) copy-start(f32[8,512]{1,0:T(8,128)S(1)} %fusion.50) | copy-start | bytes 49156
  108.7 63.7 %copy-start.28 = (f32[8,512]{1,0:T(8,128)S(1)}, f32[8,512]{1,0:T(8,128)}, u32[]{:S(2)}) copy-start(f32[8,512]{1,0:T(8,128)} %copy-done.27) | copy-start | bytes 49156
  173.7 69.6 %copy-start.8 = (f32[8,512]{1,0:T(8,128)}, f32[8,512]{1,0:T(8,128)S(1)}, u32[]{:S(2)}) copy-start(f32[8,512]{1,0:T(8,128)S(1)} %convolution_add_fusion.31) | copy-start | bytes 49156
  175.6 68.6 %copy-start.41 = (f32[128]{0:T(128)S(1)}, f32[128]{0:T(128)}, u32[]{:S(2)}) copy-start(f32[128]{0:T(128)} %copy-done.39) | copy-start | bytes 1540
  248.0 40.5 %copy-start.19 = (f32[8,512]{1,0:T(8,128)}, f32[8,512]{1,0:T(8,128)S(1)}, u32[]{:S(2)}) copy-start(f32[8,512]{1,0:T(8,128)S(1)} %fusion.44) | copy-start | bytes 49156
  248.2 40.3 %copy-start.22 = (f32[8,512]{1,0:T(8,128)}, f32[8,512]{1,0:T(8,128)S(1)}, u32[]{:S(2)}) copy-start(f32[8,512]{1,0:T(8,128)S(1)} %fusion.48) | copy-start | bytes 49156
  249.2 63.2 %copy-start.1 = (f32[128,512]{1,0:T(8,128)S(1)}, f32[128,512]{1,0:T(8,128)}, u32[]{:S(2)}) copy-start(f32[128,512]{1,0:T(8,128)} %copy-done) | copy-start | bytes 786436
  249.2 63.2 %copy-start.51 = (f32[128]{0:T(128)S(1)}, f32[128]{0:T(128)}, u32[]{:S(2)}) copy-start(f32[128]{0:T(128)} %copy-done.48) | copy-start | bytes 1540
  249.2 63.2 %copy-start.54 = (f32[8,128]{1,0:T(8,128)S(1)}, f32[8,128]{1,0:T(8,128)}, u32[]{:S(2)}) copy-start(f32[8,128]{1,0:T(8,128)} %fusion.91) | copy-start | bytes 12292
  249.2 63.3 %copy-start.47 = (f32[128]{0:T(128)S(1)}, f32[128]{0:T(128)}, u32[]{:S(2)}) copy-start(f32[128]{0:T(128)} %copy-done.44) | copy-start | bytes 1540
  249.2 63.5 %copy-start.43 = (f32[128]{0:T(128)S(1)}, f32[128]{0:T(128)}, u32[]{:S(2)}) copy-start(f32[128]{0:T(128)} %copy-done.39) | copy-start | bytes 1540
  249.2 63.7 %copy-start.38 = (f32[128]{0:T(128)S(1)}, f32[128]{0:T(128)}, u32[]{:S(2)}) copy-start(f32[128]{0:T(128)} %copy-done.36) | copy-start | bytes 1540
  249.2 63.8 %copy-start.35 = (f32[128]{0:T(128)S(1)}, f32[128]{0:T(128)}, u32[]{:S(2)}) copy-start(f32[128]{0:T(128)} %copy-done.33) | copy-start | bytes 1540
  249.2 64.2 %copy-start.4 = (f32[128,512]{1,0:T(8,128)S(1)}, f32[128,512]{1,0:T(8,128)}, u32[]{:S(2)}) copy-start(f32[128,512]{1,0:T(8,128)} %copy-done.2) | copy-start | bytes 786436
  249.2 64.2 %copy-start.56 = (f32[128]{0:T(128)S(1)}, f32[128]{0:T(128)}, u32[]{:S(2)}) copy-start(f32[128]{0:T(128)} %copy-done.55) | copy-start | bytes 1540
  252.6 58.5 %copy-start.16 = (f32[8,512]{1,0:T(8,128)S(1)}, f32[8,512]{1,0:T(8,128)}, u32[]{:S(2)}) copy-start(f32[8,512]{1,0:T(8,128)} %copy-done.15) | copy-start | bytes 49156
  288.6 78.1 %copy-start.7 = (f32[128,512]{1,0:T(8,128)S(1)}, f32[128,512]{1,0:T(8,128)}, u32[]{:S(2)}) copy-start(f32[128,512]{1,0:T(8,128)} %copy-done.5) | copy-start | bytes 786436
  (38 other events, 375.2 us)
Sparse Core Ops, SparseCore 0:
  19.8 22.6 all-reduce.2
Sparse Core Ops, SparseCore 1:
  41.7 58.3 all-gather.10
  102.7 54.4 all-gather.8
where the time goes:
time: 382 us; the launch traced here: 377 us
  blocking collectives  155 us (41%)
  matrix products  110 us (29%)
  waiting for transfers between devices  46.2 us (12%)
  between operations  38.1 us (10%)
  local copies, waits for them, and re-layouts  18 us (5%)
  other arithmetic  9.39 us (2%)
    all_gather x4, blocking collectives, carried_in(): pieces = jax.tree.map(lambda part: lax.all_gather(part, axis), value)  155 us
    dot_general x60, matrix products, compose(): moved = jnp.dot(former[1], latter[0], precision=highest) + latter[1]  60.7 us
    all_gather x2, waiting for transfers between devices, carried_in(): pieces = jax.tree.map(lambda part: lax.all_gather(part, axis), value)  46.1 us
    dot_general x16, matrix products, shards(): jnp.dot(link_coefficient[segment][None, :] * running, core_rows[segment],...  16.6 us
    dot_general x16, matrix products, shards(): jnp.dot(running, core_rows[segment], precision=highest)  8.75 us
    dot_general x15, matrix products, shards(): jnp.dot(forward_tail, forward_steps[segment], precision=highest)  8.38 us
  transfers between devices with their start and end apart: 3, of which 1 were waited for; matrix products, arithmetic and copies ran while one was open for 9% of the time, Pallas kernels for 0%

commit v1 on v0

v1 whole, which is shorter than its diff:
```python
import functools

import jax
import jax.numpy as jnp
from jax import lax
from jax.experimental import pallas as pl
from jax.experimental.pallas import tpu as pltpu
from jax.sharding import PartitionSpec as P

HOURS = 2
GROUP = 4
clock_timestep = 1.0
level_step = 0.1
bf16 = jnp.bfloat16
f32 = jnp.float32
MESH = pl.DeviceIdType.MESH


def split(x):
    high = x.astype(bf16)
    return high, (x - high.astype(f32)).astype(bf16)


def pack(matrix):
    high, low = split(matrix)
    return jnp.concatenate(
        [
            jnp.concatenate([high, low], axis=1),
            jnp.concatenate([high, jnp.zeros_like(low)], axis=1),
        ],
        axis=0,
    )


def mm3(x, tile):
    high = x.astype(bf16).astype(f32)
    both = jnp.concatenate([high, x - high], axis=1).astype(bf16)
    y = jnp.dot(both, tile, preferred_element_type=f32)
    half = y.shape[1] // 2
    return y[:, :half] + y[:, half:]


def mm3_split(x, high_matrix, low_matrix):
    rows = x.shape[0]
    high = x.astype(bf16).astype(f32)
    both = jnp.concatenate([high, x - high], axis=0).astype(bf16)
    y = jnp.dot(both, high_matrix, preferred_element_type=f32)
    return (
        y[:rows]
        + y[rows:]
        + jnp.dot(high.astype(bf16), low_matrix, preferred_element_type=f32)
    )


def kernel(
    n_route,
    n_scen,
    start_ref,
    schur_hbm,
    link_ref,
    class_ref,
    diss_hbm,
    holder_ref,
    square_ref,
    out_ref,
    schur,
    low_stack,
    core_tile,
    row_high,
    row_low,
    links,
    classes,
    class_smem,
    diss,
    tails_out,
    tails,
    carry_out,
    carry_in,
    core_first,
    z_high,
    z_low,
    dev_tile,
    grp_tile,
    part,
    z_local,
    solved_ref,
    schur_sem,
    link_send,
    link_recv,
    class_send,
    class_recv,
    class_sem,
    diss_sem,
    diss_send,
    diss_recv,
    tail_send,
    tail_recv,
    carry_send,
    carry_recv,
):
    segments, cases, nodes = start_ref.shape
    core = link_ref.shape[1]
    class_count = schur.shape[0]
    circuits = diss.shape[2]
    n_groups = n_route // GROUP
    route = lax.axis_index("route")
    scen = lax.axis_index("scen")
    place = lax.rem(route, GROUP)
    group = lax.div(route, GROUP)
    base = group * GROUP

    def mate(k):
        return {"route": base + lax.rem(place + k, GROUP)}

    def other(k):
        return {"scen": lax.rem(scen + k, n_scen)}

    later = {"route": lax.rem(route + GROUP, n_route)}
    former = {"route": lax.rem(route + n_route - GROUP, n_route)}

    core_copy = pltpu.make_async_copy(
        schur_hbm.at[:, pl.ds(0, core), pl.ds(0, core)], core_first, schur_sem.at[0]
    )
    core_copy.start()
    schur_copy = pltpu.make_async_copy(schur_hbm, schur, schur_sem.at[1])
    schur_copy.start()
    own_diss = pltpu.make_async_copy(diss_hbm.at[0], diss.at[scen], diss_sem)
    own_diss.start()

    barrier = pltpu.get_barrier_semaphore()
    for k in range(1, GROUP):
        pl.semaphore_signal(barrier, inc=1, device_id=mate(k), device_id_type=MESH)
    for k in range(1, n_scen):
        pl.semaphore_signal(barrier, inc=1, device_id=other(k), device_id_type=MESH)
    pl.semaphore_signal(barrier, inc=1, device_id=later, device_id_type=MESH)
    pl.semaphore_signal(barrier, inc=1, device_id=former, device_id_type=MESH)
    pl.semaphore_wait(barrier, GROUP + n_scen)

    def send(src, dst, send_sem, recv_sem, device):
        return pltpu.make_async_remote_copy(
            src_ref=src,
            dst_ref=dst,
            send_sem=send_sem,
            recv_sem=recv_sem,
            device_id=device,
            device_id_type=MESH,
        )

    link_copies = []
    for k in range(1, GROUP):
        slot = GROUP - k
        link_copies.append(
            send(link_ref, links.at[slot], link_send.at[k], link_recv.at[slot], mate(k))
        )
        link_copies.append(
            send(class_ref, classes.at[slot], class_send.at[k], class_recv.at[slot], mate(k))
        )
    for copy in link_copies:
        copy.start()
    diss_copies = []
    for k in range(1, n_scen):
        diss_copies.append(
            send(
                diss_hbm.at[0],
                diss.at[scen],
                diss_send.at[k],
                diss_recv.at[scen],
                other(k),
            )
        )
    for copy in diss_copies:
        copy.start()

    links[0] = link_ref[...]
    classes[0] = class_ref[...]
    core_copy.wait()
    for c in range(class_count):
        core_tile[c] = pack(core_first[c])
    for copy in link_copies:
        copy.wait()
    class_copy = pltpu.make_async_copy(classes, class_smem, class_sem)
    class_copy.start()
    class_copy.wait()

    rows_at = lax.broadcasted_iota(jnp.int32, (core, core), 0)
    eye = jnp.where(rows_at == lax.broadcasted_iota(jnp.int32, (core, core), 1), 1.0, 0.0)
    scaled = [[None] * segments for _ in range(GROUP)]
    reached = [[None] * segments for _ in range(GROUP)]
    for i in range(segments):
        for j in range(GROUP):
            line = links[j, i : i + 1, :]
            scaled[j][i] = (eye if i == 0 else reached[j][i - 1]) * line
            reached[j][i] = mm3(scaled[j][i], core_tile[class_smem[j, i, 0]])
    from_u = [None] * GROUP
    from_w = [eye] * GROUP
    for i in reversed(range(segments)):
        for j in range(GROUP):
            line = links[j, i : i + 1, :]
            if j == 0:
                first = scaled[j][i] if from_u[j] is None else scaled[j][i] + from_u[j]
                response = jnp.concatenate([first, from_w[j]], axis=0)
                high, low = split(response)
                z_high[:, i * core : (i + 1) * core] = high
                z_low[:, i * core : (i + 1) * core] = low
            tile = core_tile[class_smem[j, i, 0]]
            if from_u[j] is None:
                from_u[j] = reached[j][i] * line
                from_w[j] = mm3(from_w[j], tile) * line
            else:
                both = mm3(jnp.concatenate([from_u[j], from_w[j]], axis=0), tile)
                from_u[j] = (reached[j][i] + both[:core]) * line
                from_w[j] = both[core:] * line
    for j in range(GROUP):
        dev_tile[j, 0] = pack(reached[j][segments - 1])
        dev_tile[j, 1] = pack(from_u[j])
        dev_tile[j, 2] = pack(from_w[j])

    def slot_of(j):
        return lax.rem(j - place + GROUP, GROUP)

    u = eye
    us = []
    mine = jnp.zeros((core, core), f32)
    for j in range(GROUP):
        us.append(u)
        mine = jnp.where(place == j, u, mine)
        u = mm3(u, dev_tile[slot_of(j), 0])
    grp_tile[0] = pack(u)
    grp_tile[3] = pack(mine)
    wu = jnp.zeros((core, core), f32)
    ww = eye
    mine_u = jnp.zeros((core, core), f32)
    mine_w = jnp.zeros((core, core), f32)
    for j in reversed(range(GROUP)):
        mine_u = jnp.where(place == j, wu, mine_u)
        mine_w = jnp.where(place == j, ww, mine_w)
        both = mm3(jnp.concatenate([wu, ww], axis=0), dev_tile[slot_of(j), 2])
        wu = both[:core] + mm3(us[j], dev_tile[slot_of(j), 1])
        ww = both[core:]
    grp_tile[1] = pack(wu)
    grp_tile[2] = pack(ww)
    grp_tile[4] = pack(mine_u)
    grp_tile[5] = pack(mine_w)

    schur_copy.wait()
    for c in range(class_count):
        low_stack[c * nodes : (c + 1) * nodes, :] = schur[c].astype(bf16)
        high, low = split(schur[c, :core, :])
        row_high[c * core : (c + 1) * core, :] = high
        row_low[c * core : (c + 1) * core, :] = low
    own_diss.wait()
    for copy in diss_copies:
        copy.wait_send()
    for k in range(1, n_scen):
        source = lax.rem(scen + k, n_scen)
        send(
            diss_hbm.at[0], diss.at[source], diss_send.at[k], diss_recv.at[source], other(k)
        ).wait_recv()

    count = segments * cases
    row_class = jnp.broadcast_to(
        class_ref[...][:, None, :], (segments, cases, core)
    ).reshape(count, core)[:, :1]

    def by_class(x):
        return jnp.concatenate(
            [jnp.where(row_class == c, x, 0.0) for c in range(class_count)], axis=1
        )

    tail_sends = []
    for hour in range(HOURS):
        before = start_ref[...] if hour == 0 else out_ref[hour - 1]
        squares = square_ref[hour]
        power = None
        for c in range(circuits):
            block = diss[holder_ref[hour, c], :, c, :]
            term = squares[:, c : c + 1][None] * block[:, None, :]
            power = term if power is None else power + term
        driving = (before + clock_timestep * power).reshape(count, nodes)
        driving = driving.astype(bf16).astype(f32)
        solved = jnp.dot(
            by_class(driving).astype(bf16), low_stack[...], preferred_element_type=f32
        )
        solved_ref[...] = solved

        u = None
        entering = []
        reach = []
        for i in range(segments):
            line = link_ref[i : i + 1, :]
            own = solved[i * cases : (i + 1) * cases, :core]
            if u is None:
                entering.append(None)
                u = own
            else:
                entering.append(u * line)
                u = own + mm3(entering[i], core_tile[class_smem[0, i, 0]])
            reach.append(u)
        w = None
        for i in reversed(range(segments)):
            line = link_ref[i : i + 1, :]
            if w is None:
                z_local[i] = entering[i] if entering[i] is not None else jnp.zeros_like(u)
                w = reach[i] * line
            else:
                z_local[i] = w if entering[i] is None else entering[i] + w
                w = (reach[i] + mm3(w, core_tile[class_smem[0, i, 0]])) * line
        tails[hour, 0] = jnp.concatenate([u, w], axis=0)
        tails_out[hour] = jnp.concatenate([u, w], axis=0)
        copies = []
        for k in range(1, GROUP):
            slot = GROUP - k
            copies.append(
                send(
                    tails_out.at[hour],
                    tails.at[hour, slot],
                    tail_send.at[hour, k],
                    tail_recv.at[hour, slot],
                    mate(k),
                )
            )
        for copy in copies:
            copy.start()
        for copy in copies:
            copy.wait()

        u = jnp.zeros((cases, core), f32)
        u_mine = jnp.zeros((cases, core), f32)
        us = []
        for j in range(GROUP):
            slot = slot_of(j)
            us.append(u)
            u_mine = jnp.where(place == j, u, u_mine)
            own = tails[hour, slot, :cases]
            u = own if j == 0 else own + mm3(u, dev_tile[slot, 0])
        w = jnp.zeros((cases, core), f32)
        w_mine = jnp.zeros((cases, core), f32)
        for j in reversed(range(GROUP)):
            slot = slot_of(j)
            w_mine = jnp.where(place == j, w, w_mine)
            own = tails[hour, slot, cases:]
            if j > 0:
                own = own + mm3(us[j], dev_tile[slot, 1])
            w = own if j == GROUP - 1 else own + mm3(w, dev_tile[slot, 2])

        forward_send = send(
            carry_out.at[hour, 0],
            carry_in.at[hour, 0],
            carry_send.at[hour, 0],
            carry_recv.at[hour, 0],
            later,
        )
        backward_send = send(
            carry_out.at[hour, 1],
            carry_in.at[hour, 1],
            carry_send.at[hour, 1],
            carry_recv.at[hour, 1],
            former,
        )

        @pl.when(group == 0)
        def _():
            carry_in[hour, 0] = jnp.zeros((cases, core), f32)

        @pl.when(group > 0)
        def _():
            forward_send.wait_recv()

        u_in = carry_in[hour, 0]
        carry_out[hour, 0] = u + mm3(u_in, grp_tile[0])

        @pl.when(group < n_groups - 1)
        def _():
            forward_send.start()

        w = w + mm3(u_in, grp_tile[1])
        u_mine = u_mine + mm3(u_in, grp_tile[3])
        w_mine = w_mine + mm3(u_in, grp_tile[4])

        @pl.when(group == n_groups - 1)
        def _():
            carry_in[hour, 1] = jnp.zeros((cases, core), f32)

        @pl.when(group < n_groups - 1)
        def _():
            backward_send.wait_recv()

        w_in = carry_in[hour, 1]
        carry_out[hour, 1] = w + mm3(w_in, grp_tile[2])

        @pl.when(group > 0)
        def _():
            backward_send.start()

        w_mine = w_mine + mm3(w_in, grp_tile[5])
        spread = mm3_split(
            jnp.concatenate([u_mine, w_mine], axis=1), z_high[...], z_low[...]
        )
        z = jnp.concatenate(
            [z_local[i] + spread[:, i * core : (i + 1) * core] for i in range(segments)],
            axis=0,
        )
        result = solved_ref[...] + mm3_split(by_class(z), row_high[...], row_low[...])
        out_ref[hour] = result.reshape(segments, cases, nodes)

        @pl.when(group < n_groups - 1)
        def _():
            forward_send.wait_send()

        @pl.when(group > 0)
        def _():
            backward_send.wait_send()


def shards(start, schur, groups, link, diss, holder, demand):
    segments, cases, nodes = start.shape
    core = link.shape[1]
    class_count = schur.shape[0]
    circuits = diss.shape[2]
    n_route = lax.axis_size("route")
    n_scen = lax.axis_size("scen")
    current = demand.astype(f32) * level_step
    squares = jnp.transpose(current * current, (0, 2, 1))
    class_rows = jnp.broadcast_to(groups[:, None], (segments, core))
    vmem = pl.BlockSpec(memory_space=pltpu.VMEM)
    hbm = pl.BlockSpec(memory_space=pl.ANY)
    smem = pl.BlockSpec(memory_space=pltpu.SMEM)
    dma = pltpu.SemaphoreType.DMA
    return pl.pallas_call(
        functools.partial(kernel, n_route, n_scen),
        out_shape=jax.ShapeDtypeStruct((HOURS, segments, cases, nodes), f32),
        in_specs=[vmem, hbm, vmem, vmem, hbm, smem, vmem],
        out_specs=vmem,
        scratch_shapes=[
            pltpu.VMEM((class_count, nodes, nodes), f32),
            pltpu.VMEM((class_count * nodes, nodes), bf16),
            pltpu.VMEM((class_count, 2 * core, 2 * core), bf16),
            pltpu.VMEM((class_count * core, nodes), bf16),
            pltpu.VMEM((class_count * core, nodes), bf16),
            pltpu.VMEM((GROUP, segments, core), f32),
            pltpu.VMEM((GROUP, segments, core), jnp.int32),
            pltpu.SMEM((GROUP, segments, core), jnp.int32),
            pltpu.VMEM((n_scen, segments, circuits, nodes), f32),
            pltpu.VMEM((HOURS, 2 * cases, core), f32),
            pltpu.VMEM((HOURS, GROUP, 2 * cases, core), f32),
            pltpu.VMEM((HOURS, 2, cases, core), f32),
            pltpu.VMEM((HOURS, 2, cases, core), f32),
            pltpu.VMEM((class_count, core, core), f32),
            pltpu.VMEM((2 * core, segments * core), bf16),
            pltpu.VMEM((2 * core, segments * core), bf16),
            pltpu.VMEM((GROUP, 3, 2 * core, 2 * core), bf16),
            pltpu.VMEM((6, 2 * core, 2 * core), bf16),
            pltpu.VMEM((2, cases, core), f32),
            pltpu.VMEM((segments, cases, core), f32),
            pltpu.VMEM((segments * cases, nodes), f32),
            dma((2,)),
            dma((GROUP,)),
            dma((GROUP,)),
            dma((GROUP,)),
            dma((GROUP,)),
            dma,
            dma,
            dma((n_scen,)),
            dma((n_scen,)),
            dma((HOURS, GROUP)),
            dma((HOURS, GROUP)),
            dma((HOURS, 2)),
            dma((HOURS, 2)),
        ],
        compiler_params=pltpu.CompilerParams(
            collective_id=0, has_side_effects=True, vmem_limit_bytes=40 * 1024 * 1024
        ),
    )(start, schur, link, class_rows, diss, holder, squares)


def solution(mesh):
    return jax.shard_map(
        shards,
        mesh=mesh,
        in_specs=(
            P("route", "scen", None),
            P(),
            P("route"),
            P("route", None),
            P("scen", "route", None, None),
            P(),
            P(None, None, "scen"),
        ),
        out_specs=P(None, "route", "scen", None),
        check_vma=False,
    )
```

time: 382 us -> 70.3 us (0.18); the launches traced: 377 us -> 70 us
  blocking collectives: 155 us -> 0 us
  matrix products: 110 us -> 0 us
  Pallas kernels: 0 us -> 62.3 us
  waiting for transfers between devices: 46.2 us -> 0 us
  between operations: 38.1 us -> 0.02 us
  local copies, waits for them, and re-layouts: 18 us -> 7.61 us
  other arithmetic: 9.39 us -> 0.01 us
    all_gather x4 -> x0, blocking collectives: 155 us -> none  [carried_in(): pieces = jax.tree.map(lambda part: lax.all_gather(part, axis), value)]
    dot_general x154 -> x0, matrix products: 110 us -> none  [the longest x60 60.7 us: compose(): moved = jnp.dot(former[1], latter[0], precision=highest) + latter[1]]
    pallas_call x0 -> x1, Pallas kernels: none -> 62.3 us  [shards(): pl.pallas_call(functools.partial(kernel, n_route, n_scen), out_shape=jax....]
    all_gather x2 -> x0, waiting for transfers between devices: 46.1 us -> none  [carried_in(): pieces = jax.tree.map(lambda part: lax.all_gather(part, axis), value)]
    slice x4 -> x0, local copies, waits for them, and re-layouts: 5.39 us -> none  [the longest x1 1.94 us: shards(): lax.dynamic_index_in_dim(schur_reciprocal, ground_level_group[segment], 0...]
    convert_element_type x3 -> x0, other arithmetic: 4.32 us -> none  [the longest x1 2.46 us: shards(): inverse_low = schur_reciprocal.astype(jnp.bfloat16)]
  transfers between devices with their start and end apart: 3 -> 0, of which waited for: 1 -> 0; matrix products, arithmetic and copies ran while one was open for 9% -> 0% of each run, Pallas kernels for 0% -> 0%
where the time goes in v1:
time: 70.3 us; the launch traced here: 70 us
  Pallas kernels  62.3 us (89%)
  local copies, waits for them, and re-layouts  7.61 us (11%)
    pallas_call x1, Pallas kernels, shards(): pl.pallas_call(functools.partial(kernel, n_route, n_scen), out_shape=jax....  62.3 us
    unnamed x11, local copies, waits for them, and re-layouts  6.88 us

profile of v1, /device:TPU:0, one launch (start us, length us, event | category | flops | bytes accessed | tf_op | source)
XLA Modules:
  0.0 70.0 jit_solution(1732127266217860342)
XLA Ops:
  0.0 0.7 %broadcast_in_dim.2.class_ref = s32[8,128]{1,0:T(8,128)S(1)} broadcast(s32[8]{0:T(128)} %param.9), dimensions={0} | broadcast | bytes 4128 | tf_op jit(solution)/shard_map/broadcast_in_dim | solution.py:424
  0.7 0.8 %copy.8 = s32[2,6,8]{1,2,0:T(8,128)S(1)} copy(s32[2,6,8]{2,0,1:T(2,128)} %param.13) | data formatting | bytes 768 | tf_op args[6]
  1.5 1.0 %copy.9.diss_hbm = f32[1,8,6,512]{3,2,1,0:T(8,128)S(1)} copy(f32[1,8,6,512]{3,1,2,0:T(8,128)} %param.11) | data formatting | bytes 196608 | tf_op args[4]
  2.5 0.0 copy-start
  2.5 2.2 %copy-done = f32[4,512,512]{2,1,0:T(8,128)S(1)} copy-done((f32[4,512,512]{2,1,0:T(8,128)S(1)}, f32[4,512,512]{2,1,0:T(8,128)}, u32[]{:S(2)}) %copy-start) | copy-done | bytes 4194328
  4.7 0.0 copy-start.1
  4.7 0.9 %copy-done.1 = f32[8,8,512]{2,1,0:T(8,128)S(1)} copy-done((f32[8,8,512]{2,1,0:T(8,128)S(1)}, f32[8,8,512]{2,1,0:T(8,128)}, u32[]{:S(2)}) %copy-start.1) | copy-done | bytes 131096
  5.6 0.0 copy-start.2
  5.6 0.7 copy-done.2
  6.2 0.0 copy-start.3
  6.2 0.7 copy-done.3
  6.9 62.3 %shard_map.73 = f32[2,8,8,512]{3,2,1,0:T(8,128)S(1)} custom-call(f32[8,8,512]{2,1,0:T(8,128)S(1)} %copy-done.1, f32[4,512,512]{2,1,0:T(8,128)S(1)} %copy-done, f32[8,128]{1,0:T(8,128)S(1)} %copy-done.2, s32[8,128]{1,0:T(8,128)S(1)} %broadcast_in_dim.2.class_ref, f32[1,8,6,512]{3,2,1,0:T(8,128)S(1)} %copy.9.diss_hbm, s32[2,6]{1,0:T(2,128)S(1)} %copy-done.3, ...), custom_call_target="tpu_custom_call" | custom-call | tf_op jit(solution)/shard_map/pallas_call | solution.py:429
  69.3 0.7 %copy.11 = f32[2,8,8,512]{3,2,1,0:T(8,128)} copy(f32[2,8,8,512]{3,2,1,0:T(8,128)S(1)} %shard_map.73) | data formatting | bytes 524288
  (1 shorter events, 0.0 us)
Async XLA Ops:
  2.5 2.2 %copy-start = (f32[4,512,512]{2,1,0:T(8,128)S(1)}, f32[4,512,512]{2,1,0:T(8,128)}, u32[]{:S(2)}) copy-start(f32[4,512,512]{2,1,0:T(8,128)} %schur_hbm.1) | copy-start | bytes 12582916
  4.7 0.9 %copy-start.1 = (f32[8,8,512]{2,1,0:T(8,128)S(1)}, f32[8,8,512]{2,1,0:T(8,128)}, u32[]{:S(2)}) copy-start(f32[8,8,512]{2,1,0:T(8,128)} %start_ref.1) | copy-start | bytes 393220
  5.6 0.7 copy-start.2
  6.2 0.7 copy-start.3

commit v2 on v1

v2 whole, which is shorter than its diff:
```python
import functools

import jax
import jax.numpy as jnp
from jax import lax
from jax.experimental import pallas as pl
from jax.experimental.pallas import tpu as pltpu
from jax.sharding import PartitionSpec as P

HOURS = 2
SUB = 4
clock_timestep = 1.0
level_step = 0.1
bf16 = jnp.bfloat16
f32 = jnp.float32
MESH = pl.DeviceIdType.MESH


def split(x):
    high = x.astype(bf16)
    return high, (x - high.astype(f32)).astype(bf16)


def pack(matrix):
    high, low = split(matrix)
    return jnp.concatenate(
        [
            jnp.concatenate([high, low], axis=1),
            jnp.concatenate([high, jnp.zeros_like(low)], axis=1),
        ],
        axis=0,
    )


def mm3(x, tile):
    high = x.astype(bf16).astype(f32)
    both = jnp.concatenate([high, x - high], axis=1).astype(bf16)
    y = jnp.dot(both, tile, preferred_element_type=f32)
    half = y.shape[1] // 2
    return y[:, :half] + y[:, half:]


def mm3_split(x, high_matrix, low_matrix):
    rows = x.shape[0]
    high = x.astype(bf16).astype(f32)
    both = jnp.concatenate([high, x - high], axis=0).astype(bf16)
    y = jnp.dot(both, high_matrix, preferred_element_type=f32)
    return (
        y[:rows]
        + y[rows:]
        + jnp.dot(high.astype(bf16), low_matrix, preferred_element_type=f32)
    )


def kernel(
    n_route,
    n_scen,
    start_hbm,
    schur_hbm,
    link_hbm,
    class_hbm,
    diss_hbm,
    holder_hbm,
    demand_hbm,
    out_ref,
    start_ref,
    schur,
    low_stack,
    core_tile,
    row_high,
    row_low,
    links,
    classes,
    class_smem,
    holder_ref,
    demand,
    diss,
    tails_out,
    tails,
    core_first,
    z_high,
    z_low,
    dev_mat,
    dev_tile,
    sub_tile,
    own_tile,
    z_local,
    solved_ref,
    local_sem,
    link_send,
    link_recv,
    class_send,
    class_recv,
    diss_send,
    diss_recv,
    mat_send,
    mat_recv,
    tail_send,
    tail_recv,
):
    segments, cases, nodes = start_ref.shape
    core = links.shape[2]
    class_count = schur.shape[0]
    circuits = diss.shape[1]
    share = n_route // n_scen
    n_sub = n_route // SUB
    route = lax.axis_index("route")
    scen = lax.axis_index("scen")

    def mate(k):
        return {"route": lax.rem(route + k, n_route)}

    def other(k):
        return {"scen": lax.rem(scen + k, n_scen)}

    def local(src, dst, index):
        copy = pltpu.make_async_copy(src, dst, local_sem.at[index])
        copy.start()
        return copy

    core_copy = local(schur_hbm.at[:, pl.ds(0, core), pl.ds(0, core)], core_first, 0)
    link_copy = local(link_hbm, links.at[route], 1)
    class_copy = local(class_hbm, classes.at[route], 2)
    own_class_copy = local(class_hbm, class_smem.at[route], 3)
    schur_copy = local(schur_hbm, schur, 4)
    start_copy = local(start_hbm, start_ref, 5)
    holder_copy = local(holder_hbm, holder_ref, 6)
    demand_copy = local(demand_hbm, demand, 7)
    own_diss = local(diss_hbm.at[0], diss.at[scen], 8)

    barrier = pltpu.get_barrier_semaphore()
    for k in range(1, n_scen):
        pl.semaphore_signal(barrier, inc=1, device_id=other(k), device_id_type=MESH)
    for k in range(1, n_route):
        pl.semaphore_signal(barrier, inc=1, device_id=mate(k), device_id_type=MESH)
    pl.semaphore_wait(barrier, n_route + n_scen - 2)

    def send(src, dst, send_sem, recv_sem, device):
        return pltpu.make_async_remote_copy(
            src_ref=src,
            dst_ref=dst,
            send_sem=send_sem,
            recv_sem=recv_sem,
            device_id=device,
            device_id_type=MESH,
        )

    def diss_send_to(k, source):
        return send(
            diss_hbm.at[0], diss.at[source], diss_send.at[k], diss_recv.at[source], other(k)
        )

    def link_send_to(k, source):
        return send(
            link_hbm, links.at[source], link_send.at[k], link_recv.at[source], mate(k)
        )

    def class_send_to(k, source):
        return send(
            class_hbm, classes.at[source], class_send.at[k], class_recv.at[source], mate(k)
        )

    def tail_send_to(hour, k, source):
        return send(
            tails_out.at[hour],
            tails.at[hour, source],
            tail_send.at[hour, k],
            tail_recv.at[hour, source],
            mate(k),
        )

    for k in range(1, n_scen):
        diss_send_to(k, scen).start()
    for k in range(1, n_route):
        link_send_to(k, route).start()
        class_send_to(k, route).start()

    core_copy.wait()
    for c in range(class_count):
        core_tile[c] = pack(core_first[c])
    schur_copy.wait()
    for c in range(class_count):
        low_stack[c * nodes : (c + 1) * nodes, :] = schur[c].astype(bf16)
        high, low = split(schur[c, :core, :])
        row_high[c * core : (c + 1) * core, :] = high
        row_low[c * core : (c + 1) * core, :] = low
    link_copy.wait()
    class_copy.wait()
    own_class_copy.wait()
    start_copy.wait()
    holder_copy.wait()
    demand_copy.wait()
    own_diss.wait()

    count = segments * cases
    row_class = jnp.broadcast_to(
        classes[route][:, None, :], (segments, cases, core)
    ).reshape(count, core)[:, :1]

    def by_class(x):
        return jnp.concatenate(
            [jnp.where(row_class == c, x, 0.0) for c in range(class_count)], axis=1
        )

    levels = demand[...].astype(f32) * level_step
    squares = levels * levels
    on_diagonal = lax.broadcasted_iota(
        jnp.int32, (cases, cases), 0
    ) == lax.broadcasted_iota(jnp.int32, (cases, cases), 1)

    def local_part(hour, before):
        power = None
        for c in range(circuits):
            row = jnp.broadcast_to(squares[c, hour : hour + 1, :], (cases, cases))
            factor = jnp.sum(jnp.where(on_diagonal, row, 0.0), axis=1, keepdims=True)
            block = diss[holder_ref[hour, c], c]
            term = factor[None] * block[:, None, :]
            power = term if power is None else power + term
        driving = (before + clock_timestep * power).reshape(count, nodes)
        driving = driving.astype(bf16).astype(f32)
        solved = jnp.dot(
            by_class(driving).astype(bf16), low_stack[...], preferred_element_type=f32
        )
        solved_ref[...] = solved
        u = None
        entering = []
        reach = []
        for i in range(segments):
            line = links[route, i : i + 1, :]
            own = solved[i * cases : (i + 1) * cases, :core]
            if u is None:
                entering.append(None)
                u = own
            else:
                entering.append(u * line)
                u = own + mm3(entering[i], core_tile[class_smem[route, i, 0]])
            reach.append(u)
        w = None
        for i in reversed(range(segments)):
            line = links[route, i : i + 1, :]
            if w is None:
                z_local[i] = entering[i] if entering[i] is not None else jnp.zeros_like(u)
                w = reach[i] * line
            else:
                z_local[i] = w if entering[i] is None else entering[i] + w
                w = (reach[i] + mm3(w, core_tile[class_smem[route, i, 0]])) * line
        tails_out[hour] = jnp.concatenate([u, w], axis=0)
        for k in range(1, n_route):
            tail_send_to(hour, k, route).start()
        tails[hour, route] = jnp.concatenate([u, w], axis=0)

    rows_at = lax.broadcasted_iota(jnp.int32, (core, core), 0)
    eye = jnp.where(rows_at == lax.broadcasted_iota(jnp.int32, (core, core), 1), 1.0, 0.0)

    def transfer(devices, keep):
        chains = range(len(devices))
        scaled = [[None] * segments for _ in chains]
        reached = [[None] * segments for _ in chains]
        for i in range(segments):
            for j in chains:
                line = links[devices[j], i : i + 1, :]
                scaled[j][i] = (eye if i == 0 else reached[j][i - 1]) * line
                reached[j][i] = mm3(
                    scaled[j][i], core_tile[class_smem[devices[j], i, 0]]
                )
        from_u = [None] * len(devices)
        from_w = [eye] * len(devices)
        for i in reversed(range(segments)):
            for j in chains:
                line = links[devices[j], i : i + 1, :]
                if j == 0 and keep:
                    first = (
                        scaled[j][i] if from_u[j] is None else scaled[j][i] + from_u[j]
                    )
                    response = jnp.concatenate([first, from_w[j]], axis=0)
                    high, low = split(response)
                    z_high[:, i * core : (i + 1) * core] = high
                    z_low[:, i * core : (i + 1) * core] = low
                    if i == 0:
                        continue
                tile = core_tile[class_smem[devices[j], i, 0]]
                if from_u[j] is None:
                    from_u[j] = reached[j][i] * line
                    from_w[j] = mm3(from_w[j], tile) * line
                else:
                    both = mm3(jnp.concatenate([from_u[j], from_w[j]], axis=0), tile)
                    from_u[j] = (reached[j][i] + both[:core]) * line
                    from_w[j] = both[core:] * line
        return [(reached[j][segments - 1], from_u[j], from_w[j]) for j in chains]

    for k in range(1, n_scen):
        diss_send_to(k, scen).wait_send()
        diss_send_to(k, lax.rem(scen + k, n_scen)).wait_recv()

    local_part(0, start_ref[...])

    for k in range(1, n_route):
        source = lax.rem(route + k, n_route)
        link_send_to(k, route).wait_send()
        class_send_to(k, route).wait_send()
        link_send_to(k, source).wait_recv()
        class_send_to(k, source).wait_recv()
    all_class_copy = pltpu.make_async_copy(classes, class_smem, local_sem.at[2])
    all_class_copy.start()
    all_class_copy.wait()

    def mat_send_to(k, source):
        part = pl.ds(source * share, share)
        return send(
            dev_mat.at[part], dev_mat.at[part], mat_send.at[k], mat_recv.at[source], other(k)
        )

    devices = [scen * share + j for j in range(share)]
    made = transfer(devices, False)
    for j in range(share):
        for m in range(3):
            dev_mat[devices[j], m] = made[j][m]
    for k in range(1, n_scen):
        mat_send_to(k, scen).start()
    transfer([route], True)
    for j in range(share):
        for m in range(3):
            dev_tile[devices[j], m] = pack(dev_mat[devices[j], m])
    for k in range(1, n_scen):
        source = lax.rem(scen + k, n_scen)
        mat_send_to(k, source).wait_recv()
        for j in range(share):
            for m in range(3):
                dev_tile[source * share + j, m] = pack(dev_mat[source * share + j, m])
    for k in range(1, n_scen):
        mat_send_to(k, scen).wait_send()

    mine = [jnp.zeros((core, core), f32)] * 3
    us = [[eye] for _ in range(n_sub)]
    for j in range(SUB):
        for q in range(n_sub):
            d = q * SUB + j
            u = us[q][j]
            mine[0] = jnp.where(route == d, u, mine[0])
            us[q].append(dev_mat[d, 0] if j == 0 else mm3(u, dev_tile[d, 0]))
    for q in range(n_sub):
        sub_tile[q, 0] = pack(us[q][SUB])
    wu = [jnp.zeros((core, core), f32)] * n_sub
    ww = [eye] * n_sub
    for j in reversed(range(SUB)):
        for q in range(n_sub):
            d = q * SUB + j
            mine[1] = jnp.where(route == d, wu[q], mine[1])
            mine[2] = jnp.where(route == d, ww[q], mine[2])
            turn = dev_mat[d, 1] if j == 0 else mm3(us[q][j], dev_tile[d, 1])
            if j == SUB - 1:
                wu[q] = turn
                ww[q] = dev_mat[d, 2]
            else:
                both = mm3(jnp.concatenate([wu[q], ww[q]], axis=0), dev_tile[d, 2])
                wu[q] = both[:core] + turn
                ww[q] = both[core:]
    for q in range(n_sub):
        sub_tile[q, 1] = pack(wu[q])
        sub_tile[q, 2] = pack(ww[q])
    for m in range(3):
        own_tile[m] = pack(mine[m])

    zero = jnp.zeros((cases, core), f32)

    def finish(hour):
        for k in range(1, n_route):
            tail_send_to(hour, k, route).wait_send()
            tail_send_to(hour, k, lax.rem(route + k, n_route)).wait_recv()
        u_mine = zero
        us = [[zero] for _ in range(n_sub)]
        for j in range(SUB):
            for q in range(n_sub):
                d = q * SUB + j
                u = us[q][j]
                u_mine = jnp.where(route == d, u, u_mine)
                own = tails[hour, d, :cases]
                us[q].append(own if j == 0 else own + mm3(u, dev_tile[d, 0]))
        w_mine = zero
        ws = [zero] * n_sub
        for j in reversed(range(SUB)):
            for q in range(n_sub):
                d = q * SUB + j
                w_mine = jnp.where(route == d, ws[q], w_mine)
                own = tails[hour, d, cases:]
                if j > 0:
                    own = own + mm3(us[q][j], dev_tile[d, 1])
                ws[q] = own if j == SUB - 1 else own + mm3(ws[q], dev_tile[d, 2])
        run = lax.div(route, SUB)
        u = zero
        u_run = zero
        w_run = zero
        ends = []
        for q in range(n_sub):
            u_run = jnp.where(run == q, u, u_run)
            ends.append(ws[q] if q == 0 else ws[q] + mm3(u, sub_tile[q, 1]))
            u = us[q][SUB] if q == 0 else us[q][SUB] + mm3(u, sub_tile[q, 0])
        w = zero
        for q in reversed(range(n_sub)):
            w_run = jnp.where(run == q, w, w_run)
            w = ends[q] if q == n_sub - 1 else ends[q] + mm3(w, sub_tile[q, 2])
        u_mine = u_mine + mm3(u_run, own_tile[0])
        w_mine = w_mine + mm3(u_run, own_tile[1]) + mm3(w_run, own_tile[2])
        spread = mm3_split(
            jnp.concatenate([u_mine, w_mine], axis=1), z_high[...], z_low[...]
        )
        z = jnp.concatenate(
            [z_local[i] + spread[:, i * core : (i + 1) * core] for i in range(segments)],
            axis=0,
        )
        result = solved_ref[...] + mm3_split(by_class(z), row_high[...], row_low[...])
        result = result.reshape(segments, cases, nodes)
        out_ref[hour] = result
        return result

    result = finish(0)
    for hour in range(1, HOURS):
        local_part(hour, result)
        result = finish(hour)


def shards(start, schur, groups, link, diss, holder, demand):
    segments, cases, nodes = start.shape
    core = link.shape[1]
    class_count = schur.shape[0]
    circuits = diss.shape[2]
    n_route = lax.axis_size("route")
    n_scen = lax.axis_size("scen")
    class_rows = jnp.broadcast_to(groups[:, None], (segments, core))
    by_circuit = jnp.transpose(diss, (0, 2, 1, 3))
    demand = jnp.transpose(demand, (1, 0, 2))
    hbm = pl.BlockSpec(memory_space=pltpu.HBM)
    dma = pltpu.SemaphoreType.DMA
    mebibytes = 62
    return pl.pallas_call(
        functools.partial(kernel, n_route, n_scen),
        out_shape=jax.ShapeDtypeStruct((HOURS, segments, cases, nodes), f32),
        in_specs=[hbm] * 7,
        out_specs=pl.BlockSpec(memory_space=pltpu.VMEM),
        scratch_shapes=[
            pltpu.VMEM((segments, cases, nodes), f32),
            pltpu.VMEM((class_count, nodes, nodes), f32),
            pltpu.VMEM((class_count * nodes, nodes), bf16),
            pltpu.VMEM((class_count, 2 * core, 2 * core), bf16),
            pltpu.VMEM((class_count * core, nodes), bf16),
            pltpu.VMEM((class_count * core, nodes), bf16),
            pltpu.VMEM((n_route, segments, core), f32),
            pltpu.VMEM((n_route, segments, core), jnp.int32),
            pltpu.SMEM((n_route, segments, core), jnp.int32),
            pltpu.SMEM(holder.shape, jnp.int32),
            pltpu.VMEM(demand.shape, jnp.int32),
            pltpu.VMEM((n_scen, circuits, segments, nodes), f32),
            pltpu.VMEM((HOURS, 2 * cases, core), f32),
            pltpu.VMEM((HOURS, n_route, 2 * cases, core), f32),
            pltpu.VMEM((class_count, core, core), f32),
            pltpu.VMEM((2 * core, segments * core), bf16),
            pltpu.VMEM((2 * core, segments * core), bf16),
            pltpu.VMEM((n_route, 3, core, core), f32),
            pltpu.VMEM((n_route, 3, 2 * core, 2 * core), bf16),
            pltpu.VMEM((n_route // SUB, 3, 2 * core, 2 * core), bf16),
            pltpu.VMEM((3, 2 * core, 2 * core), bf16),
            pltpu.VMEM((segments, cases, core), f32),
            pltpu.VMEM((segments * cases, nodes), f32),
            dma((9,)),
            dma((n_route,)),
            dma((n_route,)),
            dma((n_route,)),
            dma((n_route,)),
            dma((n_scen,)),
            dma((n_scen,)),
            dma((n_scen,)),
            dma((n_scen,)),
            dma((HOURS, n_route)),
            dma((HOURS, n_route)),
        ],
        compiler_params=pltpu.CompilerParams(
            collective_id=0,
            has_side_effects=True,
            vmem_limit_bytes=mebibytes * 1024 * 1024,
        ),
    )(start, schur, link, class_rows, by_circuit, holder, demand)


def solution(mesh):
    return jax.shard_map(
        shards,
        mesh=mesh,
        in_specs=(
            P("route", "scen", None),
            P(),
            P("route"),
            P("route", None),
            P("scen", "route", None, None),
            P(),
            P(None, None, "scen"),
        ),
        out_specs=P(None, "route", "scen", None),
        check_vma=False,
    )
```

time: 70.3 us -> 38.3 us (0.54)
  Pallas kernels: 62.3 us -> 35.1 us
  local copies, waits for them, and re-layouts: 7.61 us -> 2.99 us
    pallas_call x1, Pallas kernels: 62.3 us -> 35.1 us  [shards(): pl.pallas_call(functools.partial(kernel, n_route, n_scen), out_shape=jax....]
    unnamed x11 -> x1, local copies, waits for them, and re-layouts: 6.88 us -> 1.67 us
where the time goes in v2:
time: 38.3 us; the launch traced here: 38.1 us
  Pallas kernels  35.1 us (92%)
  local copies, waits for them, and re-layouts  2.99 us (8%)
    pallas_call x1, Pallas kernels, shards(): pl.pallas_call(functools.partial(kernel, n_route, n_scen), out_shape=jax....  35.1 us
    unnamed x1, local copies, waits for them, and re-layouts  1.67 us
    broadcast_in_dim x1, local copies, waits for them, and re-layouts, shards(): class_rows = jnp.broadcast_to(groups[:, None], (segments, core))  1.31 us

profile of v2, /device:TPU:0, one launch (start us, length us, event | category | flops | bytes accessed | tf_op | source)
XLA Modules:
  0.0 38.1 jit_solution(14565299156047513583)
XLA Ops:
  0.0 1.3 %broadcast_in_dim.2.class_hbm = s32[8,128]{1,0:T(8,128)} broadcast(s32[8]{0:T(128)} %param.9), dimensions={0} | broadcast | bytes 4128 | tf_op jit(solution)/shard_map/broadcast_in_dim | solution.py:429
  1.3 35.1 %shard_map.73 = f32[2,8,8,512]{3,2,1,0:T(8,128)} custom-call(f32[8,8,512]{2,1,0:T(8,128)} %start_hbm.1, f32[4,512,512]{2,1,0:T(8,128)} %schur_hbm.1, f32[8,128]{1,0:T(8,128)} %link_hbm.1, s32[8,128]{1,0:T(8,128)} %broadcast_in_dim.2.class_hbm, f32[1,6,8,512]{3,2,1,0:T(8,128)} %bitcast.2, s32[2,6]{1,0:T(2,128)} %holder_hbm.1, s32[6,2,8]{2,1,0:T(2,128)} %bitcast.3), custom_call_target="tpu_custom_call" | custom-call | tf_op jit(solution)/shard_map/pallas_call | solution.py:435
  36.5 1.7 %copy.9 = f32[2,8,8,512]{3,2,1,0:T(8,128)} copy(f32[2,8,8,512]{3,2,1,0:T(8,128)} %shard_map.73) | data formatting | bytes 524288

commit v3 on v2

--- a/solution.py
+++ b/solution.py
@@ -72,6 +72,7 @@
     links,
     classes,
     class_smem,
+    own_class,
     holder_ref,
     demand,
     diss,
@@ -120,8 +121,7 @@
 
     core_copy = local(schur_hbm.at[:, pl.ds(0, core), pl.ds(0, core)], core_first, 0)
     link_copy = local(link_hbm, links.at[route], 1)
-    class_copy = local(class_hbm, classes.at[route], 2)
-    own_class_copy = local(class_hbm, class_smem.at[route], 3)
+    own_class_copy = local(class_hbm, own_class, 3)
     schur_copy = local(schur_hbm, schur, 4)
     start_copy = local(start_hbm, start_ref, 5)
     holder_copy = local(holder_hbm, holder_ref, 6)
@@ -133,6 +133,10 @@
         pl.semaphore_signal(barrier, inc=1, device_id=other(k), device_id_type=MESH)
     for k in range(1, n_route):
         pl.semaphore_signal(barrier, inc=1, device_id=mate(k), device_id_type=MESH)
+    own_class_copy.wait()
+    own_classes = [own_class[i] for i in range(segments)]
+    for i in range(segments):
+        classes[route, i : i + 1, :] = jnp.full((1, core), own_classes[i], jnp.int32)
     pl.semaphore_wait(barrier, n_route + n_scen - 2)
 
     def send(src, dst, send_sem, recv_sem, device):
@@ -157,7 +161,7 @@
 
     def class_send_to(k, source):
         return send(
-            class_hbm, classes.at[source], class_send.at[k], class_recv.at[source], mate(k)
+            classes.at[route], classes.at[source], class_send.at[k], class_recv.at[source], mate(k)
         )
 
     def tail_send_to(hour, k, source):
@@ -185,8 +189,6 @@
         row_high[c * core : (c + 1) * core, :] = high
         row_low[c * core : (c + 1) * core, :] = low
     link_copy.wait()
-    class_copy.wait()
-    own_class_copy.wait()
     start_copy.wait()
     holder_copy.wait()
     demand_copy.wait()
@@ -233,7 +235,7 @@
                 u = own
             else:
                 entering.append(u * line)
-                u = own + mm3(entering[i], core_tile[class_smem[route, i, 0]])
+                u = own + mm3(entering[i], core_tile[own_classes[i]])
             reach.append(u)
         w = None
         for i in reversed(range(segments)):
@@ -243,7 +245,7 @@
                 w = reach[i] * line
             else:
                 z_local[i] = w if entering[i] is None else entering[i] + w
-                w = (reach[i] + mm3(w, core_tile[class_smem[route, i, 0]])) * line
+                w = (reach[i] + mm3(w, core_tile[own_classes[i]])) * line
         tails_out[hour] = jnp.concatenate([u, w], axis=0)
         for k in range(1, n_route):
             tail_send_to(hour, k, route).start()
@@ -292,8 +294,6 @@
         diss_send_to(k, scen).wait_send()
         diss_send_to(k, lax.rem(scen + k, n_scen)).wait_recv()
 
-    local_part(0, start_ref[...])
-
     for k in range(1, n_route):
         source = lax.rem(route + k, n_route)
         link_send_to(k, route).wait_send()
@@ -302,6 +302,8 @@
         class_send_to(k, source).wait_recv()
     all_class_copy = pltpu.make_async_copy(classes, class_smem, local_sem.at[2])
     all_class_copy.start()
+    local_part(0, start_ref[...])
+
     all_class_copy.wait()
 
     def mat_send_to(k, source):
@@ -426,7 +428,6 @@
     circuits = diss.shape[2]
     n_route = lax.axis_size("route")
     n_scen = lax.axis_size("scen")
-    class_rows = jnp.broadcast_to(groups[:, None], (segments, core))
     by_circuit = jnp.transpose(diss, (0, 2, 1, 3))
     demand = jnp.transpose(demand, (1, 0, 2))
     hbm = pl.BlockSpec(memory_space=pltpu.HBM)
@@ -447,6 +448,7 @@
             pltpu.VMEM((n_route, segments, core), f32),
             pltpu.VMEM((n_route, segments, core), jnp.int32),
             pltpu.SMEM((n_route, segments, core), jnp.int32),
+            pltpu.SMEM((segments,), jnp.int32),
             pltpu.SMEM(holder.shape, jnp.int32),
             pltpu.VMEM(demand.shape, jnp.int32),
             pltpu.VMEM((n_scen, circuits, segments, nodes), f32),
@@ -478,7 +480,7 @@
             has_side_effects=True,
             vmem_limit_bytes=mebibytes * 1024 * 1024,
         ),
-    )(start, schur, link, class_rows, by_circuit, holder, demand)
+    )(start, schur, link, groups, by_circuit, holder, demand)
 
 
 def solution(mesh):

time: 38.3 us -> 39 us (1.018)
  Pallas kernels: 35.1 us -> 37.2 us
  local copies, waits for them, and re-layouts: 2.99 us -> 1.67 us
    pallas_call x1, Pallas kernels: 35.1 us -> 37.2 us  [shards(): pl.pallas_call(functools.partial(kernel, n_route, n_scen), out_shape=jax....]
    broadcast_in_dim x1 -> x0, local copies, waits for them, and re-layouts: 1.31 us -> none  [shards(): class_rows = jnp.broadcast_to(groups[:, None], (segments, core))]
where the time goes in v3:
time: 39 us; the launch traced here: 38.8 us
  Pallas kernels  37.2 us (95%)
  local copies, waits for them, and re-layouts  1.67 us (4%)
    pallas_call x1, Pallas kernels, shards(): pl.pallas_call(functools.partial(kernel, n_route, n_scen), out_shape=jax....  37.2 us
    unnamed x1, local copies, waits for them, and re-layouts  1.67 us

profile of v3, /device:TPU:0, one launch (start us, length us, event | category | flops | bytes accessed | tf_op | source)
XLA Modules:
  0.0 38.8 jit_solution(487517767856192443)
XLA Ops:
  0.0 37.2 %shard_map.73 = f32[2,8,8,512]{3,2,1,0:T(8,128)} custom-call(f32[8,8,512]{2,1,0:T(8,128)} %start_hbm.1, f32[4,512,512]{2,1,0:T(8,128)} %schur_hbm.1, f32[8,128]{1,0:T(8,128)} %link_hbm.1, s32[8]{0:T(128)} %class_hbm.1, f32[1,6,8,512]{3,2,1,0:T(8,128)} %bitcast.2, s32[2,6]{1,0:T(2,128)} %holder_hbm.1, s32[6,2,8]{2,1,0:T(2,128)} %bitcast.3), custom_call_target="tpu_custom_call" | custom-call | tf_op jit(solution)/shard_map/pallas_call | solution.py:436
  37.2 1.7 %copy.9 = f32[2,8,8,512]{3,2,1,0:T(8,128)} copy(f32[2,8,8,512]{3,2,1,0:T(8,128)} %shard_map.73) | data formatting | bytes 524288
